TPU v7x, 32 devices: a whole 2x2x4 slice. The times are simulated.
32 devices in a mesh: parts: 2 (over y), span: 4 (over x, core), seq: 4 (over z).
Axes of the slice: x: 2, y: 2, z: 4, core: 2. Of those that a mesh axis runs over, the one named last changes fastest.
Arguments:
- q_in: bfloat16 [8, 1024, 4096], P(('parts', 'span'), 'seq'), parts along dimension 0, may hold values from -9 to 9
- k_in: bfloat16 [8, 1024, 4096], P(('parts', 'span'), 'seq'), parts along dimension 0, may hold values from -9 to 9
- v_in: bfloat16 [8, 1024, 4096], P(('parts', 'span'), 'seq'), parts along dimension 0, may hold values from -18 to 18
- timesteps: int32 [8], P('parts'), parts along dimension 0, may hold values from 0 to 31
- gate_table: float32 [32, 4096], replicated, may hold values from 0.1 to 1.9
Outputs:
- gated_out: bfloat16 [8, 1024, 4096], P(('parts', 'span'), 'seq'), parts along dimension 0
There are 2 independent parts, one for each index of `parts`. A program takes and returns all parts, laid end to end along the dimension named above; an argument that names none is the same for every part. Nothing has to cross between parts.
All inputs are finite; a program needn't handle non-finite values.
Results may differ from a plain program's by a relative error of at most 0.0053.
Values may be sent and summed in bfloat16 or wider, within the bound.
A program may use at most 128 MiB of HBM per device.

v0:
```python
import math
import jax
import jax.numpy as jnp
from jax import lax
from jax.sharding import PartitionSpec as P

HD = 128
masked_score = -1e30


def local(q_in, k_in, v_in, timesteps, gate_table):
    head_rows, key_rows, value_rows = (
        lax.all_to_all(q_in[0], "seq", split_axis=1, concat_axis=0, tiled=True),
        lax.all_to_all(k_in[0], "seq", split_axis=1, concat_axis=0, tiled=True),
        lax.all_to_all(v_in[0], "seq", split_axis=1, concat_axis=0, tiled=True),
    )
    length = head_rows.shape[0]
    columns = head_rows.shape[1]
    heads = columns // HD
    scale = HD ** (-0.5)
    span_id = lax.axis_index("span")
    limit = (span_id + 1) * length
    query_three = head_rows.reshape(length, heads, HD)
    init = (
        jnp.full((heads, length), masked_score, jnp.float32),
        jnp.zeros((heads, length), jnp.float32),
        jnp.zeros((length, heads, HD), jnp.float32),
    )
    key_piece = lax.all_gather(key_rows, "span", axis=0, tiled=True)
    value_piece = lax.all_gather(value_rows, "span", axis=0, tiled=True)
    count = key_piece.shape[0]
    block = math.gcd(count, 512)

    def one_block(index, state):
        top, total, accum = state
        offset = index * block
        key_block = lax.dynamic_slice_in_dim(key_piece, offset, block, 0).reshape(block, heads, HD)
        value_block = lax.dynamic_slice_in_dim(value_piece, offset, block, 0).reshape(
            block, heads, HD
        )
        scores = (
            jnp.einsum("qhd,khd->hqk", query_three, key_block, preferred_element_type=jnp.float32)
            * scale
        )
        keep = offset + jnp.arange(block) < limit
        scores = jnp.where(keep[None, None, :], scores, masked_score)
        new_top = jnp.maximum(top, jnp.max(scores, axis=-1))
        expo = jnp.where(keep[None, None, :], jnp.exp(scores - new_top[:, :, None]), 0.0)
        shrink = jnp.exp(top - new_top)
        total = total * shrink + jnp.sum(expo, axis=-1)
        mixed = jnp.einsum(
            "hqk,khd->qhd",
            expo.astype(jnp.bfloat16),
            value_block,
            preferred_element_type=jnp.float32,
        )
        accum = accum * shrink.T[:, :, None] + mixed
        return (new_top, total, accum)

    def run_blocks(state):
        return lax.fori_loop(0, count // block, one_block, state)

    def keep_state(state):
        return state

    top, total, accum = lax.cond(jnp.int32(0) < limit, run_blocks, keep_state, init)
    attn = (accum / total.T[:, :, None]).reshape(length, columns).astype(jnp.bfloat16)
    token_rows = lax.all_to_all(attn, "seq", split_axis=0, concat_axis=1, tiled=True)
    steps_count = gate_table.shape[0]
    span_step = lax.dynamic_index_in_dim(timesteps, span_id, 0, keepdims=False)
    picked = (jnp.arange(steps_count) == span_step).astype(jnp.float32)
    gate = jnp.dot(picked, gate_table, precision=lax.Precision.HIGHEST)
    return (token_rows.astype(jnp.float32) * gate[None, :]).astype(jnp.bfloat16)[None]


def solution(mesh):
    in_specs = (
        P(("parts", "span"), "seq", None),
        P(("parts", "span"), "seq", None),
        P(("parts", "span"), "seq", None),
        P("parts"),
        P(),
    )
    out_specs = P(("parts", "span"), "seq", None)
    return jax.shard_map(local, mesh=mesh, in_specs=in_specs, out_specs=out_specs, check_vma=False)
```

profile of v0, /device:TPU:0, one launch (start us, length us, event | category | flops | bytes accessed | tf_op | source)
XLA Modules:
  0.0 533.7 jit_solution(13859830746761117424)
XLA Ops:
  10.7 54.5 %all_to_all.64 = bf16[256,4,1024]{0,2,1:T(8,128)(2,1)S(1)} all-to-all(bf16[256,4,1024]{0,2,1:T(8,128)(2,1)} %bitcast.80), channel_id=1, replica_groups=mesh['parts'=2,'span'=4,'seq'=4] {'seq'}, dimensions={1} | all-to-all | bytes 4194304 | tf_op jit(solution)/shard_map/all_to_all | solution.py:14
  71.8 51.0 %all_to_all.65 = bf16[256,4,1024]{0,2,1:T(8,128)(2,1)S(1)} all-to-all(bf16[256,4,1024]{0,2,1:T(8,128)(2,1)} %bitcast.81), channel_id=1, replica_groups=mesh['parts'=2,'span'=4,'seq'=4] {'seq'}, dimensions={1} | all-to-all | bytes 4194304 | tf_op jit(solution)/shard_map/all_to_all | solution.py:15
  132.9 47.3 %all-to-all-done = bf16[256,4,1024]{0,2,1:T(8,128)(2,1)S(1)} async-done(((bf16[256,4,1024]{0,2,1:T(8,128)(2,1)}), bf16[256,4,1024]{0,2,1:T(8,128)(2,1)S(1)}, u32[]{:S(2)}, u32[]{:S(2)}) %all-to-all-start) | async-done | bytes 2097184 | tf_op jit(solution)/shard_map/all_to_all | solution.py:13
  180.2 5.0 all-gather.5.cloned.1.call-done
  185.2 271.6 %conditional.1 = (f32[8,1024]{1,0:T(8,128)}, f32[1024,8,128]{0,2,1:T(8,128)}) conditional(s32[]{:T(128)} %convert_element_type.44, () %tuple.27, (bf16[4,256,1024]{1,2,0:T(8,128)(2,1)S(1)}, s32[]{:T(128)}, bf16[4096,1024]{1,0:T(8,128)(2,1)}, bf16[4096,1024]{1,0:T(8,128)(2,1)}) %tuple.65), branch_computations={%region_0.0_spmd, %region_1.6_spmd} | conditional | flops 2205205504 | bytes 151521616 | solution.py:66
  191.5 265.3 %while.17 = (s32[]{:T(128)}, f32[8,1024]{1,0:T(8,128)S(1)}, f32[8,1024]{1,0:T(8,128)}, f32[1024,8,128]{0,2,1:T(8,128)}, s32[]{:T(128)}, /*index=5*/bf16[4096,102...) while((s32[]{:T(128)}, f32[8,1024]{1,0:T(8,128)S(1)}, ...), condition=%wide.region_5.5_spmd.clone, body=%wide.region_2.4_spmd.clone.sunk | while | flops 2205205504 | bytes 138938576 | solution.py:61
  195.7 9.4 %bitcast_reduce_fusion.2 = (f32[8,1024]{1,0:T(8,128)S(1)}, f32[8,512,1024]{2,1,0:T(8,128)}) fusion(pred[512]{0:T(512)(128)(4,1)S(1)} %add_compare_fusion.2, bf16[512,8,128]{0,2,1:T(8,128)(2,1)S(1)} %bitcast.72, bf16[1024,8,128]{2,0,1:T(8,128)(2,1)} %get-tuple-element.338), kind=kOutput, calls=%fused_computation.1.clone.1 | convolution fusion | flops 1086316544 | bytes 19956224 | tf_op jit(solution)/shard_map/cond/branch_1_fun/while/body/eval_jaxpr/qhd,khd->hqk/dot_general | solution.py:42
  205.6 10.9 %bitcast_add_fusion.2 = f32[1024,8,128]{0,2,1:T(8,128)} fusion(f32[1024,8,128]{0,2,1:T(8,128)} %get-tuple-element.323, bf16[512,8,128]{0,2,1:T(8,128)(2,1)S(1)} %bitcast.73, f32[8,512,1024]{2,1,0:T(8,128)} %get-tuple-element.305, f32[8,1024]{1,0:T(8,128)S(1)} %get-tuple-element.333, pred[512]{0:T(512)(128)(4,1)S(1)} %add_compare_fusion.2, ...), kind=kOutput, calls=%fused_computation.10.clone.1 | convolution fusion | flops 1097859072 | bytes 26280448 | tf_op jit(solution)/shard_map/cond/branch_1_fun/while/body/eval_jaxpr/hqk,khd->qhd/dot_general | solution.py:51
  217.7 4.6 fusion.37
  227.1 9.4 %bitcast_reduce_fusion.2 = (f32[8,1024]{1,0:T(8,128)S(1)}, f32[8,512,1024]{2,1,0:T(8,128)}) fusion(pred[512]{0:T(512)(128)(4,1)S(1)} %add_compare_fusion.2, bf16[512,8,128]{0,2,1:T(8,128)(2,1)S(1)} %bitcast.72, bf16[1024,8,128]{2,0,1:T(8,128)(2,1)} %get-tuple-element.338), kind=kOutput, calls=%fused_computation.1.clone.1 | convolution fusion | flops 1086316544 | bytes 19956224 | tf_op jit(solution)/shard_map/cond/branch_1_fun/while/body/eval_jaxpr/qhd,khd->hqk/dot_general | solution.py:42
  237.1 12.1 %bitcast_add_fusion.2 = f32[1024,8,128]{0,2,1:T(8,128)} fusion(f32[1024,8,128]{0,2,1:T(8,128)} %get-tuple-element.323, bf16[512,8,128]{0,2,1:T(8,128)(2,1)S(1)} %bitcast.73, f32[8,512,1024]{2,1,0:T(8,128)} %get-tuple-element.305, f32[8,1024]{1,0:T(8,128)S(1)} %get-tuple-element.333, pred[512]{0:T(512)(128)(4,1)S(1)} %add_compare_fusion.2, ...), kind=kOutput, calls=%fused_computation.10.clone.1 | convolution fusion | flops 1097859072 | bytes 26280448 | tf_op jit(solution)/shard_map/cond/branch_1_fun/while/body/eval_jaxpr/hqk,khd->qhd/dot_general | solution.py:51
  250.3 4.6 fusion.37
  260.5 9.4 %bitcast_reduce_fusion.2 = (f32[8,1024]{1,0:T(8,128)S(1)}, f32[8,512,1024]{2,1,0:T(8,128)}) fusion(pred[512]{0:T(512)(128)(4,1)S(1)} %add_compare_fusion.2, bf16[512,8,128]{0,2,1:T(8,128)(2,1)S(1)} %bitcast.72, bf16[1024,8,128]{2,0,1:T(8,128)(2,1)} %get-tuple-element.338), kind=kOutput, calls=%fused_computation.1.clone.1 | convolution fusion | flops 1086316544 | bytes 19956224 | tf_op jit(solution)/shard_map/cond/branch_1_fun/while/body/eval_jaxpr/qhd,khd->hqk/dot_general | solution.py:42
  270.5 12.1 %bitcast_add_fusion.2 = f32[1024,8,128]{0,2,1:T(8,128)} fusion(f32[1024,8,128]{0,2,1:T(8,128)} %get-tuple-element.323, bf16[512,8,128]{0,2,1:T(8,128)(2,1)S(1)} %bitcast.73, f32[8,512,1024]{2,1,0:T(8,128)} %get-tuple-element.305, f32[8,1024]{1,0:T(8,128)S(1)} %get-tuple-element.333, pred[512]{0:T(512)(128)(4,1)S(1)} %add_compare_fusion.2, ...), kind=kOutput, calls=%fused_computation.10.clone.1 | convolution fusion | flops 1097859072 | bytes 26280448 | tf_op jit(solution)/shard_map/cond/branch_1_fun/while/body/eval_jaxpr/hqk,khd->qhd/dot_general | solution.py:51
  283.7 4.6 fusion.37
  293.9 9.4 %bitcast_reduce_fusion.2 = (f32[8,1024]{1,0:T(8,128)S(1)}, f32[8,512,1024]{2,1,0:T(8,128)}) fusion(pred[512]{0:T(512)(128)(4,1)S(1)} %add_compare_fusion.2, bf16[512,8,128]{0,2,1:T(8,128)(2,1)S(1)} %bitcast.72, bf16[1024,8,128]{2,0,1:T(8,128)(2,1)} %get-tuple-element.338), kind=kOutput, calls=%fused_computation.1.clone.1 | convolution fusion | flops 1086316544 | bytes 19956224 | tf_op jit(solution)/shard_map/cond/branch_1_fun/while/body/eval_jaxpr/qhd,khd->hqk/dot_general | solution.py:42
  303.9 12.1 %bitcast_add_fusion.2 = f32[1024,8,128]{0,2,1:T(8,128)} fusion(f32[1024,8,128]{0,2,1:T(8,128)} %get-tuple-element.323, bf16[512,8,128]{0,2,1:T(8,128)(2,1)S(1)} %bitcast.73, f32[8,512,1024]{2,1,0:T(8,128)} %get-tuple-element.305, f32[8,1024]{1,0:T(8,128)S(1)} %get-tuple-element.333, pred[512]{0:T(512)(128)(4,1)S(1)} %add_compare_fusion.2, ...), kind=kOutput, calls=%fused_computation.10.clone.1 | convolution fusion | flops 1097859072 | bytes 26280448 | tf_op jit(solution)/shard_map/cond/branch_1_fun/while/body/eval_jaxpr/hqk,khd->qhd/dot_general | solution.py:51
  317.1 4.6 fusion.37
  327.4 9.4 %bitcast_reduce_fusion.2 = (f32[8,1024]{1,0:T(8,128)S(1)}, f32[8,512,1024]{2,1,0:T(8,128)}) fusion(pred[512]{0:T(512)(128)(4,1)S(1)} %add_compare_fusion.2, bf16[512,8,128]{0,2,1:T(8,128)(2,1)S(1)} %bitcast.72, bf16[1024,8,128]{2,0,1:T(8,128)(2,1)} %get-tuple-element.338), kind=kOutput, calls=%fused_computation.1.clone.1 | convolution fusion | flops 1086316544 | bytes 19956224 | tf_op jit(solution)/shard_map/cond/branch_1_fun/while/body/eval_jaxpr/qhd,khd->hqk/dot_general | solution.py:42
  337.3 12.1 %bitcast_add_fusion.2 = f32[1024,8,128]{0,2,1:T(8,128)} fusion(f32[1024,8,128]{0,2,1:T(8,128)} %get-tuple-element.323, bf16[512,8,128]{0,2,1:T(8,128)(2,1)S(1)} %bitcast.73, f32[8,512,1024]{2,1,0:T(8,128)} %get-tuple-element.305, f32[8,1024]{1,0:T(8,128)S(1)} %get-tuple-element.333, pred[512]{0:T(512)(128)(4,1)S(1)} %add_compare_fusion.2, ...), kind=kOutput, calls=%fused_computation.10.clone.1 | convolution fusion | flops 1097859072 | bytes 26280448 | tf_op jit(solution)/shard_map/cond/branch_1_fun/while/body/eval_jaxpr/hqk,khd->qhd/dot_general | solution.py:51
  350.5 4.6 fusion.37
  360.8 9.4 %bitcast_reduce_fusion.2 = (f32[8,1024]{1,0:T(8,128)S(1)}, f32[8,512,1024]{2,1,0:T(8,128)}) fusion(pred[512]{0:T(512)(128)(4,1)S(1)} %add_compare_fusion.2, bf16[512,8,128]{0,2,1:T(8,128)(2,1)S(1)} %bitcast.72, bf16[1024,8,128]{2,0,1:T(8,128)(2,1)} %get-tuple-element.338), kind=kOutput, calls=%fused_computation.1.clone.1 | convolution fusion | flops 1086316544 | bytes 19956224 | tf_op jit(solution)/shard_map/cond/branch_1_fun/while/body/eval_jaxpr/qhd,khd->hqk/dot_general | solution.py:42
  370.7 12.1 %bitcast_add_fusion.2 = f32[1024,8,128]{0,2,1:T(8,128)} fusion(f32[1024,8,128]{0,2,1:T(8,128)} %get-tuple-element.323, bf16[512,8,128]{0,2,1:T(8,128)(2,1)S(1)} %bitcast.73, f32[8,512,1024]{2,1,0:T(8,128)} %get-tuple-element.305, f32[8,1024]{1,0:T(8,128)S(1)} %get-tuple-element.333, pred[512]{0:T(512)(128)(4,1)S(1)} %add_compare_fusion.2, ...), kind=kOutput, calls=%fused_computation.10.clone.1 | convolution fusion | flops 1097859072 | bytes 26280448 | tf_op jit(solution)/shard_map/cond/branch_1_fun/while/body/eval_jaxpr/hqk,khd->qhd/dot_general | solution.py:51
  383.9 4.6 fusion.37
  394.2 9.4 %bitcast_reduce_fusion.2 = (f32[8,1024]{1,0:T(8,128)S(1)}, f32[8,512,1024]{2,1,0:T(8,128)}) fusion(pred[512]{0:T(512)(128)(4,1)S(1)} %add_compare_fusion.2, bf16[512,8,128]{0,2,1:T(8,128)(2,1)S(1)} %bitcast.72, bf16[1024,8,128]{2,0,1:T(8,128)(2,1)} %get-tuple-element.338), kind=kOutput, calls=%fused_computation.1.clone.1 | convolution fusion | flops 1086316544 | bytes 19956224 | tf_op jit(solution)/shard_map/cond/branch_1_fun/while/body/eval_jaxpr/qhd,khd->hqk/dot_general | solution.py:42
  404.1 12.1 %bitcast_add_fusion.2 = f32[1024,8,128]{0,2,1:T(8,128)} fusion(f32[1024,8,128]{0,2,1:T(8,128)} %get-tuple-element.323, bf16[512,8,128]{0,2,1:T(8,128)(2,1)S(1)} %bitcast.73, f32[8,512,1024]{2,1,0:T(8,128)} %get-tuple-element.305, f32[8,1024]{1,0:T(8,128)S(1)} %get-tuple-element.333, pred[512]{0:T(512)(128)(4,1)S(1)} %add_compare_fusion.2, ...), kind=kOutput, calls=%fused_computation.10.clone.1 | convolution fusion | flops 1097859072 | bytes 26280448 | tf_op jit(solution)/shard_map/cond/branch_1_fun/while/body/eval_jaxpr/hqk,khd->qhd/dot_general | solution.py:51
  417.4 4.6 fusion.37
  427.6 9.4 %bitcast_reduce_fusion.2 = (f32[8,1024]{1,0:T(8,128)S(1)}, f32[8,512,1024]{2,1,0:T(8,128)}) fusion(pred[512]{0:T(512)(128)(4,1)S(1)} %add_compare_fusion.2, bf16[512,8,128]{0,2,1:T(8,128)(2,1)S(1)} %bitcast.72, bf16[1024,8,128]{2,0,1:T(8,128)(2,1)} %get-tuple-element.338), kind=kOutput, calls=%fused_computation.1.clone.1 | convolution fusion | flops 1086316544 | bytes 19956224 | tf_op jit(solution)/shard_map/cond/branch_1_fun/while/body/eval_jaxpr/qhd,khd->hqk/dot_general | solution.py:42
  437.5 12.1 %bitcast_add_fusion.2 = f32[1024,8,128]{0,2,1:T(8,128)} fusion(f32[1024,8,128]{0,2,1:T(8,128)} %get-tuple-element.323, bf16[512,8,128]{0,2,1:T(8,128)(2,1)S(1)} %bitcast.73, f32[8,512,1024]{2,1,0:T(8,128)} %get-tuple-element.305, f32[8,1024]{1,0:T(8,128)S(1)} %get-tuple-element.333, pred[512]{0:T(512)(128)(4,1)S(1)} %add_compare_fusion.2, ...), kind=kOutput, calls=%fused_computation.10.clone.1 | convolution fusion | flops 1097859072 | bytes 26280448 | tf_op jit(solution)/shard_map/cond/branch_1_fun/while/body/eval_jaxpr/hqk,khd->qhd/dot_general | solution.py:51
  450.8 4.6 fusion.37
  466.7 4.6 all-to-all-start.3
  472.8 47.3 %all-to-all-done.3 = bf16[4,256,1024]{2,1,0:T(8,128)(2,1)} async-done(((bf16[4,256,1024]{2,1,0:T(8,128)(2,1)}), bf16[4,256,1024]{2,1,0:T(8,128)(2,1)}, u32[]{:S(2)}, u32[]{:S(2)}) %all-to-all-start.3) | async-done | bytes 2097184 | tf_op jit(solution)/shard_map/all_to_all | solution.py:68
  (102 shorter events, 103.1 us)
Async XLA Ops:
  6.5 465.3 %copy-start = (f32[32,4096]{1,0:T(8,128)S(1)}, f32[32,4096]{1,0:T(8,128)}, u32[]{:S(2)}) copy-start(f32[32,4096]{1,0:T(8,128)} %param.13) | copy-start | bytes 1572868
  6.5 173.7 %all-gather.3.cloned.1.call-start = ((), (), s32[]{:S(2)}) async-start(), calls=%async_computation.4 | async-start | bytes 10485760 | tf_op jit(solution)/shard_map/all_gather | solution.py:29
  67.7 117.5 %all-gather.5.cloned.1.call-start = ((), (), s32[]{:S(2)}) async-start(), calls=%async_computation.5 | async-start | bytes 10485760 | tf_op jit(solution)/shard_map/all_gather | solution.py:30
  129.3 50.9 %all-to-all-start = ((bf16[256,4,1024]{0,2,1:T(8,128)(2,1)}), bf16[256,4,1024]{0,2,1:T(8,128)(2,1)S(1)}, u32[]{:S(2)}, u32[]{:S(2)}) async-start(bf16[256,4,1024]{0,2,1:T(8,128)(2,1)} %bitcast.78), calls=%async_computation | async-start | bytes 4194304 | tf_op jit(solution)/shard_map/all_to_all | solution.py:13
  205.6 12.1 %copy-start.1 = (f32[8,512,1024]{2,1,0:T(8,128)S(1)}, f32[8,512,1024]{2,1,0:T(8,128)}, u32[]{:S(2)}) copy-start(f32[8,512,1024]{2,1,0:T(8,128)} %get-tuple-element.305) | copy-start | bytes 50331652 | tf_op jit(solution)/shard_map/cond/branch_1_fun/while
  237.1 13.3 %copy-start.1 = (f32[8,512,1024]{2,1,0:T(8,128)S(1)}, f32[8,512,1024]{2,1,0:T(8,128)}, u32[]{:S(2)}) copy-start(f32[8,512,1024]{2,1,0:T(8,128)} %get-tuple-element.305) | copy-start | bytes 50331652 | tf_op jit(solution)/shard_map/cond/branch_1_fun/while
  270.5 13.3 %copy-start.1 = (f32[8,512,1024]{2,1,0:T(8,128)S(1)}, f32[8,512,1024]{2,1,0:T(8,128)}, u32[]{:S(2)}) copy-start(f32[8,512,1024]{2,1,0:T(8,128)} %get-tuple-element.305) | copy-start | bytes 50331652 | tf_op jit(solution)/shard_map/cond/branch_1_fun/while
  303.9 13.3 %copy-start.1 = (f32[8,512,1024]{2,1,0:T(8,128)S(1)}, f32[8,512,1024]{2,1,0:T(8,128)}, u32[]{:S(2)}) copy-start(f32[8,512,1024]{2,1,0:T(8,128)} %get-tuple-element.305) | copy-start | bytes 50331652 | tf_op jit(solution)/shard_map/cond/branch_1_fun/while
  337.3 13.3 %copy-start.1 = (f32[8,512,1024]{2,1,0:T(8,128)S(1)}, f32[8,512,1024]{2,1,0:T(8,128)}, u32[]{:S(2)}) copy-start(f32[8,512,1024]{2,1,0:T(8,128)} %get-tuple-element.305) | copy-start | bytes 50331652 | tf_op jit(solution)/shard_map/cond/branch_1_fun/while
  370.7 13.3 %copy-start.1 = (f32[8,512,1024]{2,1,0:T(8,128)S(1)}, f32[8,512,1024]{2,1,0:T(8,128)}, u32[]{:S(2)}) copy-start(f32[8,512,1024]{2,1,0:T(8,128)} %get-tuple-element.305) | copy-start | bytes 50331652 | tf_op jit(solution)/shard_map/cond/branch_1_fun/while
  404.1 13.3 %copy-start.1 = (f32[8,512,1024]{2,1,0:T(8,128)S(1)}, f32[8,512,1024]{2,1,0:T(8,128)}, u32[]{:S(2)}) copy-start(f32[8,512,1024]{2,1,0:T(8,128)} %get-tuple-element.305) | copy-start | bytes 50331652 | tf_op jit(solution)/shard_map/cond/branch_1_fun/while
  437.5 13.3 %copy-start.1 = (f32[8,512,1024]{2,1,0:T(8,128)S(1)}, f32[8,512,1024]{2,1,0:T(8,128)}, u32[]{:S(2)}) copy-start(f32[8,512,1024]{2,1,0:T(8,128)} %get-tuple-element.305) | copy-start | bytes 50331652 | tf_op jit(solution)/shard_map/cond/branch_1_fun/while
  462.4 8.9 %copy-start.2 = (s32[4]{0:T(128)S(1)}, s32[4]{0:T(128)}, u32[]{:S(2)}) copy-start(s32[4]{0:T(128)} %param.12) | copy-start | bytes 52
  466.7 53.4 %all-to-all-start.3 = ((bf16[4,256,1024]{2,1,0:T(8,128)(2,1)}), bf16[4,256,1024]{2,1,0:T(8,128)(2,1)}, u32[]{:S(2)}, u32[]{:S(2)}) async-start(bf16[4,256,1024]{2,1,0:T(8,128)(2,1)} %copy.42), calls=%async_computation.3 | async-start | bytes 4194304 | tf_op jit(solution)/shard_map/all_to_all | solution.py:68
Sparse Core Ops, SparseCore 0:
  67.8 57.4 all-gather.2
  126.9 58.2 all-gather.4
where the time goes:
time: 536 us; the launch traced here: 534 us
  matrix products  171 us (32%)
  blocking collectives  105 us (20%)
  waiting for transfers between devices  99.6 us (19%)
  local copies, waits for them, and re-layouts  84 us (16%)
  other arithmetic  51.5 us (10%)
  between operations  13.5 us (3%)
  starting transfers between devices  8.25 us (2%)
    dot_general x8, matrix products, one_block(): jnp.einsum('hqk,khd->qhd', expo.astype(jnp.bfloat16), value_block, prefer...  95.3 us
    dot_general x8, matrix products, one_block(): jnp.einsum('qhd,khd->hqk', query_three, key_block, preferred_element_type...  74.9 us
    all_to_all x1, blocking collectives, local(): lax.all_to_all(k_in[0], 'seq', split_axis=1, concat_axis=0, tiled=True)  54.5 us
    all_to_all x1, blocking collectives, local(): lax.all_to_all(v_in[0], 'seq', split_axis=1, concat_axis=0, tiled=True)  51 us
    all_to_all x1, waiting for transfers between devices, local(): lax.all_to_all(q_in[0], 'seq', split_axis=1, concat_axis=0, tiled=True)  47.3 us
    all_to_all x1, waiting for transfers between devices, local(): lax.all_to_all(attn, 'seq', split_axis=0, concat_axis=1, tiled=True)  47.3 us
    reduce_sum x8, other arithmetic, one_block(): total = total * shrink + jnp.sum(expo, axis=-1)  37 us
    dynamic_slice x16, local copies, waits for them, and re-layouts, one_block(): lax.dynamic_slice_in_dim(value_piece, offset, block, 0)  25.8 us
  transfers between devices with their start and end apart: 4, of which 3 were waited for; matrix products, arithmetic and copies ran while one was open for 2% of the time, Pallas kernels for 0%

commit v1 on v0

--- a/solution.py
+++ b/solution.py
@@ -12,7 +12,12 @@
     head_rows, key_rows, value_rows = (
         lax.all_to_all(q_in[0], "seq", split_axis=1, concat_axis=0, tiled=True),
         lax.all_to_all(k_in[0], "seq", split_axis=1, concat_axis=0, tiled=True),
-        lax.all_to_all(v_in[0], "seq", split_axis=1, concat_axis=0, tiled=True),
+        jnp.concatenate(
+            lax.all_to_all(
+                jnp.stack(jnp.split(v_in[0], lax.axis_size("seq"), axis=1)), "seq", 0, 0
+            ),
+            axis=0,
+        ),
     )
     length = head_rows.shape[0]
     columns = head_rows.shape[1]

time: 536 us -> 513 us (0.957)
  local copies, waits for them, and re-layouts: 84 us -> 61 us
    dynamic_slice x16 -> x8, local copies, waits for them, and re-layouts: 25.8 us -> 11.6 us  [one_block(): lax.dynamic_slice_in_dim(value_piece, offset, block, 0)]
    while x24 -> x72, local copies, waits for them, and re-layouts: 9.48 us -> 0.18 us
    unnamed x7 -> x6, local copies, waits for them, and re-layouts: 12.3 us -> 8.16 us
    dynamic_slice x8 -> x16, local copies, waits for them, and re-layouts: 11.9 us -> 14.7 us  [one_block(): lax.dynamic_slice_in_dim(key_piece, offset, block, 0)]
where the time goes in v1:
time: 513 us; the launch traced here: 511 us
  matrix products  171 us (33%)
  blocking collectives  105 us (20%)
  waiting for transfers between devices  99.6 us (19%)
  local copies, waits for them, and re-layouts  61 us (12%)
  other arithmetic  51.8 us (10%)
  between operations  13.5 us (3%)
  starting transfers between devices  8.25 us (2%)
    dot_general x8, matrix products, one_block(): jnp.einsum('hqk,khd->qhd', expo.astype(jnp.bfloat16), value_block, prefer...  95.1 us
    dot_general x8, matrix products, one_block(): jnp.einsum('qhd,khd->hqk', query_three, key_block, preferred_element_type...  75.2 us
    all_to_all x1, blocking collectives, local(): lax.all_to_all(jnp.stack(jnp.split(v_in[0], lax.axis_size('seq'), axis=1)...  54.3 us
    all_to_all x1, blocking collectives, local(): lax.all_to_all(k_in[0], 'seq', split_axis=1, concat_axis=0, tiled=True)  51 us
    all_to_all x1, waiting for transfers between devices, local(): lax.all_to_all(q_in[0], 'seq', split_axis=1, concat_axis=0, tiled=True)  47.3 us
    all_to_all x1, waiting for transfers between devices, local(): lax.all_to_all(attn, 'seq', split_axis=0, concat_axis=1, tiled=True)  47.3 us
    reduce_sum x8, other arithmetic, one_block(): total = total * shrink + jnp.sum(expo, axis=-1)  37.1 us
    dynamic_slice x16, local copies, waits for them, and re-layouts, one_block(): lax.dynamic_slice_in_dim(key_piece, offset, block, 0)  14.7 us
  transfers between devices with their start and end apart: 4, of which 3 were waited for; matrix products, arithmetic and copies ran while one was open for 2% of the time, Pallas kernels for 0%

profile of v1, /device:TPU:0, one launch (start us, length us, event | category | flops | bytes accessed | tf_op | source)
XLA Modules:
  0.0 511.4 jit_solution(11278586858821618686)
XLA Ops:
  8.6 54.3 %all_to_all.50 = bf16[4,256,1024]{2,1,0:T(8,128)(2,1)S(1)} all-to-all(bf16[4,256,1024]{2,1,0:T(8,128)(2,1)S(1)} %pad_maximum_fusion), channel_id=1, replica_groups=mesh['parts'=2,'span'=4,'seq'=4] {'seq'}, dimensions={0} | all-to-all | bytes 4194304 | tf_op jit(solution)/shard_map/all_to_all | solution.py:16
  69.6 51.0 %all_to_all.51 = bf16[256,4,1024]{0,2,1:T(8,128)(2,1)S(1)} all-to-all(bf16[256,4,1024]{0,2,1:T(8,128)(2,1)} %bitcast.88), channel_id=1, replica_groups=mesh['parts'=2,'span'=4,'seq'=4] {'seq'}, dimensions={1} | all-to-all | bytes 4194304 | tf_op jit(solution)/shard_map/all_to_all | solution.py:14
  130.7 47.3 %all-to-all-done = bf16[256,4,1024]{0,2,1:T(8,128)(2,1)S(1)} async-done(((bf16[256,4,1024]{0,2,1:T(8,128)(2,1)}), bf16[256,4,1024]{0,2,1:T(8,128)(2,1)S(1)}, u32[]{:S(2)}, u32[]{:S(2)}) %all-to-all-start) | async-done | bytes 2097184 | tf_op jit(solution)/shard_map/all_to_all | solution.py:13
  178.0 5.0 all-gather.3.cloned.1.call-done
  183.0 251.4 %conditional.1 = (f32[8,1024]{1,0:T(8,128)}, f32[1024,8,128]{0,2,1:T(8,128)}) conditional(s32[]{:T(128)} %convert_element_type.44, () %tuple.27, (bf16[4,256,1024]{1,2,0:T(8,128)(2,1)S(1)}, s32[]{:T(128)}, bf16[4096,1024]{1,0:T(8,128)(2,1)}, bf16[4096,1024]{0,1:T(8,128)(2,1)}) %tuple.65), branch_computations={%region_0.0_spmd, %region_1.6_spmd} | conditional | flops 2205205504 | bytes 132647312 | solution.py:71
  189.3 245.1 %while.17 = (s32[]{:T(128)}, f32[8,1024]{1,0:T(8,128)S(1)}, f32[8,1024]{1,0:T(8,128)}, f32[1024,8,128]{0,2,1:T(8,128)}, s32[]{:T(128)}, /*index=5*/bf16[4096,102...) while((s32[]{:T(128)}, f32[8,1024]{1,0:T(8,128)S(1)}, ...), condition=%wide.region_5.5_spmd.clone, body=%wide.region_2.4_spmd.clone.sunk | while | flops 2205205504 | bytes 120064280 | solution.py:66
  191.1 9.4 %bitcast_reduce_fusion.2 = (f32[8,1024]{1,0:T(8,128)S(1)}, f32[8,512,1024]{2,1,0:T(8,128)}) fusion(pred[512]{0:T(512)(128)(4,1)S(1)} %add_compare_fusion.2, bf16[512,8,128]{0,2,1:T(8,128)(2,1)S(1)} %bitcast.80, bf16[1024,8,128]{2,0,1:T(8,128)(2,1)} %get-tuple-element.336), kind=kOutput, calls=%fused_computation.1.clone.1 | convolution fusion | flops 1086316544 | bytes 19956224 | tf_op jit(solution)/shard_map/cond/branch_1_fun/while/body/eval_jaxpr/qhd,khd->hqk/dot_general | solution.py:47
  202.0 10.8 %bitcast_add_fusion.2 = f32[1024,8,128]{0,2,1:T(8,128)} fusion(f32[1024,8,128]{0,2,1:T(8,128)} %get-tuple-element.321, bf16[512,8,128]{0,2,1:T(8,128)(2,1)S(1)} %bitcast.81, f32[8,512,1024]{2,1,0:T(8,128)} %get-tuple-element.304, f32[8,1024]{1,0:T(8,128)S(1)} %get-tuple-element.331, pred[512]{0:T(512)(128)(4,1)S(1)} %add_compare_fusion.2, ...), kind=kOutput, calls=%fused_computation.10.clone.1 | convolution fusion | flops 1097859072 | bytes 26280448 | tf_op jit(solution)/shard_map/cond/branch_1_fun/while/body/eval_jaxpr/hqk,khd->qhd/dot_general | solution.py:56
  212.9 4.6 fusion.37
  220.1 9.4 %bitcast_reduce_fusion.2 = (f32[8,1024]{1,0:T(8,128)S(1)}, f32[8,512,1024]{2,1,0:T(8,128)}) fusion(pred[512]{0:T(512)(128)(4,1)S(1)} %add_compare_fusion.2, bf16[512,8,128]{0,2,1:T(8,128)(2,1)S(1)} %bitcast.80, bf16[1024,8,128]{2,0,1:T(8,128)(2,1)} %get-tuple-element.336), kind=kOutput, calls=%fused_computation.1.clone.1 | convolution fusion | flops 1086316544 | bytes 19956224 | tf_op jit(solution)/shard_map/cond/branch_1_fun/while/body/eval_jaxpr/qhd,khd->hqk/dot_general | solution.py:47
  231.0 12.0 %bitcast_add_fusion.2 = f32[1024,8,128]{0,2,1:T(8,128)} fusion(f32[1024,8,128]{0,2,1:T(8,128)} %get-tuple-element.321, bf16[512,8,128]{0,2,1:T(8,128)(2,1)S(1)} %bitcast.81, f32[8,512,1024]{2,1,0:T(8,128)} %get-tuple-element.304, f32[8,1024]{1,0:T(8,128)S(1)} %get-tuple-element.331, pred[512]{0:T(512)(128)(4,1)S(1)} %add_compare_fusion.2, ...), kind=kOutput, calls=%fused_computation.10.clone.1 | convolution fusion | flops 1097859072 | bytes 26280448 | tf_op jit(solution)/shard_map/cond/branch_1_fun/while/body/eval_jaxpr/hqk,khd->qhd/dot_general | solution.py:56
  243.0 4.6 fusion.37
  251.0 9.4 %bitcast_reduce_fusion.2 = (f32[8,1024]{1,0:T(8,128)S(1)}, f32[8,512,1024]{2,1,0:T(8,128)}) fusion(pred[512]{0:T(512)(128)(4,1)S(1)} %add_compare_fusion.2, bf16[512,8,128]{0,2,1:T(8,128)(2,1)S(1)} %bitcast.80, bf16[1024,8,128]{2,0,1:T(8,128)(2,1)} %get-tuple-element.336), kind=kOutput, calls=%fused_computation.1.clone.1 | convolution fusion | flops 1086316544 | bytes 19956224 | tf_op jit(solution)/shard_map/cond/branch_1_fun/while/body/eval_jaxpr/qhd,khd->hqk/dot_general | solution.py:47
  261.9 12.0 %bitcast_add_fusion.2 = f32[1024,8,128]{0,2,1:T(8,128)} fusion(f32[1024,8,128]{0,2,1:T(8,128)} %get-tuple-element.321, bf16[512,8,128]{0,2,1:T(8,128)(2,1)S(1)} %bitcast.81, f32[8,512,1024]{2,1,0:T(8,128)} %get-tuple-element.304, f32[8,1024]{1,0:T(8,128)S(1)} %get-tuple-element.331, pred[512]{0:T(512)(128)(4,1)S(1)} %add_compare_fusion.2, ...), kind=kOutput, calls=%fused_computation.10.clone.1 | convolution fusion | flops 1097859072 | bytes 26280448 | tf_op jit(solution)/shard_map/cond/branch_1_fun/while/body/eval_jaxpr/hqk,khd->qhd/dot_general | solution.py:56
  273.9 4.6 fusion.37
  281.8 9.4 %bitcast_reduce_fusion.2 = (f32[8,1024]{1,0:T(8,128)S(1)}, f32[8,512,1024]{2,1,0:T(8,128)}) fusion(pred[512]{0:T(512)(128)(4,1)S(1)} %add_compare_fusion.2, bf16[512,8,128]{0,2,1:T(8,128)(2,1)S(1)} %bitcast.80, bf16[1024,8,128]{2,0,1:T(8,128)(2,1)} %get-tuple-element.336), kind=kOutput, calls=%fused_computation.1.clone.1 | convolution fusion | flops 1086316544 | bytes 19956224 | tf_op jit(solution)/shard_map/cond/branch_1_fun/while/body/eval_jaxpr/qhd,khd->hqk/dot_general | solution.py:47
  292.7 12.0 %bitcast_add_fusion.2 = f32[1024,8,128]{0,2,1:T(8,128)} fusion(f32[1024,8,128]{0,2,1:T(8,128)} %get-tuple-element.321, bf16[512,8,128]{0,2,1:T(8,128)(2,1)S(1)} %bitcast.81, f32[8,512,1024]{2,1,0:T(8,128)} %get-tuple-element.304, f32[8,1024]{1,0:T(8,128)S(1)} %get-tuple-element.331, pred[512]{0:T(512)(128)(4,1)S(1)} %add_compare_fusion.2, ...), kind=kOutput, calls=%fused_computation.10.clone.1 | convolution fusion | flops 1097859072 | bytes 26280448 | tf_op jit(solution)/shard_map/cond/branch_1_fun/while/body/eval_jaxpr/hqk,khd->qhd/dot_general | solution.py:56
  304.8 4.6 fusion.37
  312.7 9.4 %bitcast_reduce_fusion.2 = (f32[8,1024]{1,0:T(8,128)S(1)}, f32[8,512,1024]{2,1,0:T(8,128)}) fusion(pred[512]{0:T(512)(128)(4,1)S(1)} %add_compare_fusion.2, bf16[512,8,128]{0,2,1:T(8,128)(2,1)S(1)} %bitcast.80, bf16[1024,8,128]{2,0,1:T(8,128)(2,1)} %get-tuple-element.336), kind=kOutput, calls=%fused_computation.1.clone.1 | convolution fusion | flops 1086316544 | bytes 19956224 | tf_op jit(solution)/shard_map/cond/branch_1_fun/while/body/eval_jaxpr/qhd,khd->hqk/dot_general | solution.py:47
  323.6 12.0 %bitcast_add_fusion.2 = f32[1024,8,128]{0,2,1:T(8,128)} fusion(f32[1024,8,128]{0,2,1:T(8,128)} %get-tuple-element.321, bf16[512,8,128]{0,2,1:T(8,128)(2,1)S(1)} %bitcast.81, f32[8,512,1024]{2,1,0:T(8,128)} %get-tuple-element.304, f32[8,1024]{1,0:T(8,128)S(1)} %get-tuple-element.331, pred[512]{0:T(512)(128)(4,1)S(1)} %add_compare_fusion.2, ...), kind=kOutput, calls=%fused_computation.10.clone.1 | convolution fusion | flops 1097859072 | bytes 26280448 | tf_op jit(solution)/shard_map/cond/branch_1_fun/while/body/eval_jaxpr/hqk,khd->qhd/dot_general | solution.py:56
  335.7 4.6 fusion.37
  343.6 9.4 %bitcast_reduce_fusion.2 = (f32[8,1024]{1,0:T(8,128)S(1)}, f32[8,512,1024]{2,1,0:T(8,128)}) fusion(pred[512]{0:T(512)(128)(4,1)S(1)} %add_compare_fusion.2, bf16[512,8,128]{0,2,1:T(8,128)(2,1)S(1)} %bitcast.80, bf16[1024,8,128]{2,0,1:T(8,128)(2,1)} %get-tuple-element.336), kind=kOutput, calls=%fused_computation.1.clone.1 | convolution fusion | flops 1086316544 | bytes 19956224 | tf_op jit(solution)/shard_map/cond/branch_1_fun/while/body/eval_jaxpr/qhd,khd->hqk/dot_general | solution.py:47
  354.5 12.0 %bitcast_add_fusion.2 = f32[1024,8,128]{0,2,1:T(8,128)} fusion(f32[1024,8,128]{0,2,1:T(8,128)} %get-tuple-element.321, bf16[512,8,128]{0,2,1:T(8,128)(2,1)S(1)} %bitcast.81, f32[8,512,1024]{2,1,0:T(8,128)} %get-tuple-element.304, f32[8,1024]{1,0:T(8,128)S(1)} %get-tuple-element.331, pred[512]{0:T(512)(128)(4,1)S(1)} %add_compare_fusion.2, ...), kind=kOutput, calls=%fused_computation.10.clone.1 | convolution fusion | flops 1097859072 | bytes 26280448 | tf_op jit(solution)/shard_map/cond/branch_1_fun/while/body/eval_jaxpr/hqk,khd->qhd/dot_general | solution.py:56
  366.6 4.6 fusion.37
  374.5 9.4 %bitcast_reduce_fusion.2 = (f32[8,1024]{1,0:T(8,128)S(1)}, f32[8,512,1024]{2,1,0:T(8,128)}) fusion(pred[512]{0:T(512)(128)(4,1)S(1)} %add_compare_fusion.2, bf16[512,8,128]{0,2,1:T(8,128)(2,1)S(1)} %bitcast.80, bf16[1024,8,128]{2,0,1:T(8,128)(2,1)} %get-tuple-element.336), kind=kOutput, calls=%fused_computation.1.clone.1 | convolution fusion | flops 1086316544 | bytes 19956224 | tf_op jit(solution)/shard_map/cond/branch_1_fun/while/body/eval_jaxpr/qhd,khd->hqk/dot_general | solution.py:47
  385.4 12.0 %bitcast_add_fusion.2 = f32[1024,8,128]{0,2,1:T(8,128)} fusion(f32[1024,8,128]{0,2,1:T(8,128)} %get-tuple-element.321, bf16[512,8,128]{0,2,1:T(8,128)(2,1)S(1)} %bitcast.81, f32[8,512,1024]{2,1,0:T(8,128)} %get-tuple-element.304, f32[8,1024]{1,0:T(8,128)S(1)} %get-tuple-element.331, pred[512]{0:T(512)(128)(4,1)S(1)} %add_compare_fusion.2, ...), kind=kOutput, calls=%fused_computation.10.clone.1 | convolution fusion | flops 1097859072 | bytes 26280448 | tf_op jit(solution)/shard_map/cond/branch_1_fun/while/body/eval_jaxpr/hqk,khd->qhd/dot_general | solution.py:56
  397.5 4.6 fusion.37
  405.4 9.4 %bitcast_reduce_fusion.2 = (f32[8,1024]{1,0:T(8,128)S(1)}, f32[8,512,1024]{2,1,0:T(8,128)}) fusion(pred[512]{0:T(512)(128)(4,1)S(1)} %add_compare_fusion.2, bf16[512,8,128]{0,2,1:T(8,128)(2,1)S(1)} %bitcast.80, bf16[1024,8,128]{2,0,1:T(8,128)(2,1)} %get-tuple-element.336), kind=kOutput, calls=%fused_computation.1.clone.1 | convolution fusion | flops 1086316544 | bytes 19956224 | tf_op jit(solution)/shard_map/cond/branch_1_fun/while/body/eval_jaxpr/qhd,khd->hqk/dot_general | solution.py:47
  416.3 12.0 %bitcast_add_fusion.2 = f32[1024,8,128]{0,2,1:T(8,128)} fusion(f32[1024,8,128]{0,2,1:T(8,128)} %get-tuple-element.321, bf16[512,8,128]{0,2,1:T(8,128)(2,1)S(1)} %bitcast.81, f32[8,512,1024]{2,1,0:T(8,128)} %get-tuple-element.304, f32[8,1024]{1,0:T(8,128)S(1)} %get-tuple-element.331, pred[512]{0:T(512)(128)(4,1)S(1)} %add_compare_fusion.2, ...), kind=kOutput, calls=%fused_computation.10.clone.1 | convolution fusion | flops 1097859072 | bytes 26280448 | tf_op jit(solution)/shard_map/cond/branch_1_fun/while/body/eval_jaxpr/hqk,khd->qhd/dot_general | solution.py:56
  428.4 4.6 fusion.37
  444.3 4.6 all-to-all-start.3
  450.4 47.3 %all-to-all-done.3 = bf16[4,256,1024]{2,1,0:T(8,128)(2,1)} async-done(((bf16[4,256,1024]{2,1,0:T(8,128)(2,1)}), bf16[4,256,1024]{2,1,0:T(8,128)(2,1)}, u32[]{:S(2)}, u32[]{:S(2)}) %all-to-all-start.3) | async-done | bytes 2097184 | tf_op jit(solution)/shard_map/all_to_all | solution.py:73
  (159 shorter events, 80.3 us)
Async XLA Ops:
  6.5 443.0 %copy-start = (f32[32,4096]{1,0:T(8,128)S(1)}, f32[32,4096]{1,0:T(8,128)}, u32[]{:S(2)}) copy-start(f32[32,4096]{1,0:T(8,128)} %param.13) | copy-start | bytes 1572868
  6.5 171.5 %all-gather.5.cloned.1.call-start = ((), (), s32[]{:S(2)}) async-start(), calls=%async_computation.5 | async-start | bytes 10485760 | tf_op jit(solution)/shard_map/all_gather | solution.py:35
  65.5 117.5 %all-gather.3.cloned.1.call-start = ((), (), s32[]{:S(2)}) async-start(), calls=%async_computation.4 | async-start | bytes 10485760 | tf_op jit(solution)/shard_map/all_gather | solution.py:34
  127.1 50.9 %all-to-all-start = ((bf16[256,4,1024]{0,2,1:T(8,128)(2,1)}), bf16[256,4,1024]{0,2,1:T(8,128)(2,1)S(1)}, u32[]{:S(2)}, u32[]{:S(2)}) async-start(bf16[256,4,1024]{0,2,1:T(8,128)(2,1)} %bitcast.85), calls=%async_computation | async-start | bytes 4194304 | tf_op jit(solution)/shard_map/all_to_all | solution.py:13
  200.5 12.3 %slice-start = ((s8[16777216]{0:T(1024)(128)(4,1)}), s8[4194304]{0:T(1024)(128)(4,1)S(1)}, s32[]{:S(2)}) async-start(s8[16777216]{0:T(1024)(128)(4,1)} %bitcast.78), calls=%async_computation.6 | async-start | bytes 8388608 | tf_op jit(solution)/shard_map/cond/branch_1_fun/while
  229.5 13.5 %slice-start = ((s8[16777216]{0:T(1024)(128)(4,1)}), s8[4194304]{0:T(1024)(128)(4,1)S(1)}, s32[]{:S(2)}) async-start(s8[16777216]{0:T(1024)(128)(4,1)} %bitcast.78), calls=%async_computation.6 | async-start | bytes 8388608 | tf_op jit(solution)/shard_map/cond/branch_1_fun/while
  230.9 12.1 %slice-start.1 = ((s8[16777216]{0:T(1024)(128)(4,1)}), s8[4194304]{0:T(1024)(128)(4,1)S(1)}, s32[]{:S(2)}) async-start(s8[16777216]{0:T(1024)(128)(4,1)} %bitcast.78), calls=%async_computation.7 | async-start | bytes 8388608 | tf_op jit(solution)/shard_map/cond/branch_1_fun/while
  231.0 12.1 %slice-start.2 = ((s8[16777216]{0:T(1024)(128)(4,1)}), s8[4194304]{0:T(1024)(128)(4,1)S(1)}, s32[]{:S(2)}) async-start(s8[16777216]{0:T(1024)(128)(4,1)} %bitcast.78), calls=%async_computation.8 | async-start | bytes 8388608 | tf_op jit(solution)/shard_map/cond/branch_1_fun/while
  231.0 12.1 %slice-start.3 = ((s8[16777216]{0:T(1024)(128)(4,1)}), s8[4194304]{0:T(1024)(128)(4,1)S(1)}, s32[]{:S(2)}) async-start(s8[16777216]{0:T(1024)(128)(4,1)} %bitcast.78), calls=%async_computation.9 | async-start | bytes 8388608 | tf_op jit(solution)/shard_map/cond/branch_1_fun/while
  260.4 13.5 %slice-start = ((s8[16777216]{0:T(1024)(128)(4,1)}), s8[4194304]{0:T(1024)(128)(4,1)S(1)}, s32[]{:S(2)}) async-start(s8[16777216]{0:T(1024)(128)(4,1)} %bitcast.78), calls=%async_computation.6 | async-start | bytes 8388608 | tf_op jit(solution)/shard_map/cond/branch_1_fun/while
  261.8 12.1 %slice-start.1 = ((s8[16777216]{0:T(1024)(128)(4,1)}), s8[4194304]{0:T(1024)(128)(4,1)S(1)}, s32[]{:S(2)}) async-start(s8[16777216]{0:T(1024)(128)(4,1)} %bitcast.78), calls=%async_computation.7 | async-start | bytes 8388608 | tf_op jit(solution)/shard_map/cond/branch_1_fun/while
  261.8 12.1 %slice-start.2 = ((s8[16777216]{0:T(1024)(128)(4,1)}), s8[4194304]{0:T(1024)(128)(4,1)S(1)}, s32[]{:S(2)}) async-start(s8[16777216]{0:T(1024)(128)(4,1)} %bitcast.78), calls=%async_computation.8 | async-start | bytes 8388608 | tf_op jit(solution)/shard_map/cond/branch_1_fun/while
  261.9 12.1 %slice-start.3 = ((s8[16777216]{0:T(1024)(128)(4,1)}), s8[4194304]{0:T(1024)(128)(4,1)S(1)}, s32[]{:S(2)}) async-start(s8[16777216]{0:T(1024)(128)(4,1)} %bitcast.78), calls=%async_computation.9 | async-start | bytes 8388608 | tf_op jit(solution)/shard_map/cond/branch_1_fun/while
  291.3 13.5 %slice-start = ((s8[16777216]{0:T(1024)(128)(4,1)}), s8[4194304]{0:T(1024)(128)(4,1)S(1)}, s32[]{:S(2)}) async-start(s8[16777216]{0:T(1024)(128)(4,1)} %bitcast.78), calls=%async_computation.6 | async-start | bytes 8388608 | tf_op jit(solution)/shard_map/cond/branch_1_fun/while
  292.7 12.1 %slice-start.1 = ((s8[16777216]{0:T(1024)(128)(4,1)}), s8[4194304]{0:T(1024)(128)(4,1)S(1)}, s32[]{:S(2)}) async-start(s8[16777216]{0:T(1024)(128)(4,1)} %bitcast.78), calls=%async_computation.7 | async-start | bytes 8388608 | tf_op jit(solution)/shard_map/cond/branch_1_fun/while
  292.7 12.1 %slice-start.2 = ((s8[16777216]{0:T(1024)(128)(4,1)}), s8[4194304]{0:T(1024)(128)(4,1)S(1)}, s32[]{:S(2)}) async-start(s8[16777216]{0:T(1024)(128)(4,1)} %bitcast.78), calls=%async_computation.8 | async-start | bytes 8388608 | tf_op jit(solution)/shard_map/cond/branch_1_fun/while
  292.7 12.1 %slice-start.3 = ((s8[16777216]{0:T(1024)(128)(4,1)}), s8[4194304]{0:T(1024)(128)(4,1)S(1)}, s32[]{:S(2)}) async-start(s8[16777216]{0:T(1024)(128)(4,1)} %bitcast.78), calls=%async_computation.9 | async-start | bytes 8388608 | tf_op jit(solution)/shard_map/cond/branch_1_fun/while
  322.1 13.5 %slice-start = ((s8[16777216]{0:T(1024)(128)(4,1)}), s8[4194304]{0:T(1024)(128)(4,1)S(1)}, s32[]{:S(2)}) async-start(s8[16777216]{0:T(1024)(128)(4,1)} %bitcast.78), calls=%async_computation.6 | async-start | bytes 8388608 | tf_op jit(solution)/shard_map/cond/branch_1_fun/while
  323.6 12.1 %slice-start.1 = ((s8[16777216]{0:T(1024)(128)(4,1)}), s8[4194304]{0:T(1024)(128)(4,1)S(1)}, s32[]{:S(2)}) async-start(s8[16777216]{0:T(1024)(128)(4,1)} %bitcast.78), calls=%async_computation.7 | async-start | bytes 8388608 | tf_op jit(solution)/shard_map/cond/branch_1_fun/while
  323.6 12.1 %slice-start.2 = ((s8[16777216]{0:T(1024)(128)(4,1)}), s8[4194304]{0:T(1024)(128)(4,1)S(1)}, s32[]{:S(2)}) async-start(s8[16777216]{0:T(1024)(128)(4,1)} %bitcast.78), calls=%async_computation.8 | async-start | bytes 8388608 | tf_op jit(solution)/shard_map/cond/branch_1_fun/while
  323.6 12.1 %slice-start.3 = ((s8[16777216]{0:T(1024)(128)(4,1)}), s8[4194304]{0:T(1024)(128)(4,1)S(1)}, s32[]{:S(2)}) async-start(s8[16777216]{0:T(1024)(128)(4,1)} %bitcast.78), calls=%async_computation.9 | async-start | bytes 8388608 | tf_op jit(solution)/shard_map/cond/branch_1_fun/while
  353.0 13.5 %slice-start = ((s8[16777216]{0:T(1024)(128)(4,1)}), s8[4194304]{0:T(1024)(128)(4,1)S(1)}, s32[]{:S(2)}) async-start(s8[16777216]{0:T(1024)(128)(4,1)} %bitcast.78), calls=%async_computation.6 | async-start | bytes 8388608 | tf_op jit(solution)/shard_map/cond/branch_1_fun/while
  354.5 12.1 %slice-start.1 = ((s8[16777216]{0:T(1024)(128)(4,1)}), s8[4194304]{0:T(1024)(128)(4,1)S(1)}, s32[]{:S(2)}) async-start(s8[16777216]{0:T(1024)(128)(4,1)} %bitcast.78), calls=%async_computation.7 | async-start | bytes 8388608 | tf_op jit(solution)/shard_map/cond/branch_1_fun/while
  354.5 12.1 %slice-start.2 = ((s8[16777216]{0:T(1024)(128)(4,1)}), s8[4194304]{0:T(1024)(128)(4,1)S(1)}, s32[]{:S(2)}) async-start(s8[16777216]{0:T(1024)(128)(4,1)} %bitcast.78), calls=%async_computation.8 | async-start | bytes 8388608 | tf_op jit(solution)/shard_map/cond/branch_1_fun/while
  383.9 13.5 %slice-start = ((s8[16777216]{0:T(1024)(128)(4,1)}), s8[4194304]{0:T(1024)(128)(4,1)S(1)}, s32[]{:S(2)}) async-start(s8[16777216]{0:T(1024)(128)(4,1)} %bitcast.78), calls=%async_computation.6 | async-start | bytes 8388608 | tf_op jit(solution)/shard_map/cond/branch_1_fun/while
  385.4 12.1 %slice-start.1 = ((s8[16777216]{0:T(1024)(128)(4,1)}), s8[4194304]{0:T(1024)(128)(4,1)S(1)}, s32[]{:S(2)}) async-start(s8[16777216]{0:T(1024)(128)(4,1)} %bitcast.78), calls=%async_computation.7 | async-start | bytes 8388608 | tf_op jit(solution)/shard_map/cond/branch_1_fun/while
  385.4 12.1 %slice-start.2 = ((s8[16777216]{0:T(1024)(128)(4,1)}), s8[4194304]{0:T(1024)(128)(4,1)S(1)}, s32[]{:S(2)}) async-start(s8[16777216]{0:T(1024)(128)(4,1)} %bitcast.78), calls=%async_computation.8 | async-start | bytes 8388608 | tf_op jit(solution)/shard_map/cond/branch_1_fun/while
  385.4 12.1 %slice-start.3 = ((s8[16777216]{0:T(1024)(128)(4,1)}), s8[4194304]{0:T(1024)(128)(4,1)S(1)}, s32[]{:S(2)}) async-start(s8[16777216]{0:T(1024)(128)(4,1)} %bitcast.78), calls=%async_computation.9 | async-start | bytes 8388608 | tf_op jit(solution)/shard_map/cond/branch_1_fun/while
  414.8 13.5 %slice-start = ((s8[16777216]{0:T(1024)(128)(4,1)}), s8[4194304]{0:T(1024)(128)(4,1)S(1)}, s32[]{:S(2)}) async-start(s8[16777216]{0:T(1024)(128)(4,1)} %bitcast.78), calls=%async_computation.6 | async-start | bytes 8388608 | tf_op jit(solution)/shard_map/cond/branch_1_fun/while
  416.3 12.1 %slice-start.1 = ((s8[16777216]{0:T(1024)(128)(4,1)}), s8[4194304]{0:T(1024)(128)(4,1)S(1)}, s32[]{:S(2)}) async-start(s8[16777216]{0:T(1024)(128)(4,1)} %bitcast.78), calls=%async_computation.7 | async-start | bytes 8388608 | tf_op jit(solution)/shard_map/cond/branch_1_fun/while
  416.3 12.1 %slice-start.2 = ((s8[16777216]{0:T(1024)(128)(4,1)}), s8[4194304]{0:T(1024)(128)(4,1)S(1)}, s32[]{:S(2)}) async-start(s8[16777216]{0:T(1024)(128)(4,1)} %bitcast.78), calls=%async_computation.8 | async-start | bytes 8388608 | tf_op jit(solution)/shard_map/cond/branch_1_fun/while
  444.3 53.4 %all-to-all-start.3 = ((bf16[4,256,1024]{2,1,0:T(8,128)(2,1)}), bf16[4,256,1024]{2,1,0:T(8,128)(2,1)}, u32[]{:S(2)}, u32[]{:S(2)}) async-start(bf16[4,256,1024]{2,1,0:T(8,128)(2,1)} %copy.41), calls=%async_computation.3 | async-start | bytes 4194304 | tf_op jit(solution)/shard_map/all_to_all | solution.py:73
  (6 other events, 65.7 us)
Sparse Core Ops, SparseCore 0:
  65.6 57.4 all-gather.4
  124.7 58.2 all-gather.2
